TPU v7x, 256 devices: a whole 4x4x8 slice. The times are simulated.
256 devices in a mesh: blk: 64 (over z, x, core), grp: 4 (over y).
Axes of the slice: x: 4, y: 4, z: 8, core: 2. Of those that a mesh axis runs over, the one named last changes fastest.
Arguments:
- embeddings: bfloat16 [768, 1024, 1024], P(('blk', 'grp'))
- ranks: int32 [768, 1024], P(('blk', 'grp')), may hold values from 0 to 1048575
- block_rows: int32 [768], P(('blk', 'grp')), may hold values from 1 to 1024, as said below
- pair_list: int32 [256, 6, 2], P(('blk', 'grp')), may hold values from 1 to 5, as said below
- pair_count: int32 [256], P(('blk', 'grp')), may hold values from 1 to 6, as said below
Outputs:
- best: float32 [768, 1024], P(('blk', 'grp'))
Inputs may be any that keep to these rules, and one draw needn't show every extreme that they name: `block_rows`: A block that is not the last of its cluster has 1024 live rows. `pair_list`: the blocks fall into clusters of 1 to 3 consecutive blocks, some of exactly 3. The first pair_count entries of a device are (u, v) with 3 <= u < 6 and u - 3 < v <= u, naming two blocks of one cluster or a block with itself; over all devices they name every such pair of a cluster once, at the device of the later block; the other entries are (3, 3). `pair_count`: some device has 6 live slots.
All inputs are finite; a program needn't handle non-finite values.
Results may differ from a plain program's by a relative error of at most 0.0003.
Values may be sent and summed in bfloat16 or wider, within the bound.
No kernel may reach another device: no remote copies, remote signals or barrier semaphores. Data moves between devices by JAX's collectives and lax.ppermute only.
A program may use at most 128 MiB of HBM per device.

v0:
```python
import jax
import jax.numpy as jnp
from jax import lax
from jax.sharding import PartitionSpec as P


def passed_along(value, axis, steps):
    count = lax.axis_size(axis)
    leading, last = (max(0, -steps), min(count, count - steps))
    return lax.ppermute(value, axis, [(source, source + steps) for source in range(leading, last)])


def normalize(embeddings):
    values = embeddings.astype(jnp.float32)
    scaling = lax.rsqrt(jnp.sum(values * values, axis=-1, keepdims=True) + 1e-06)
    return (values * scaling).astype(jnp.bfloat16)


def pair_update(unit_rows, rank_rows, live_rows, maxima, first_slot, second_slot):
    left_rows = unit_rows[first_slot]
    right_rows = unit_rows[second_slot]
    similarity = lax.dot_general(
        left_rows, right_rows, (((1,), (1,)), ((), ())), preferred_element_type=jnp.float32
    )
    shifted = 1.0 + similarity
    paired = live_rows[first_slot][:, None] & live_rows[second_slot][None, :]
    rank_left = rank_rows[first_slot][:, None]
    rank_right = rank_rows[second_slot][None, :]
    row_best = jnp.max(jnp.where(paired & (rank_right < rank_left), shifted, 0.0), axis=1)
    col_best = jnp.max(jnp.where(paired & (rank_left < rank_right), shifted, 0.0), axis=0)
    maxima = maxima.at[first_slot].max(row_best)
    return maxima.at[second_slot].max(col_best)


def run_pairs(unit_rows, rank_rows, counts_rows, slot_pairs, total_pairs):
    block_rows = unit_rows.shape[1]
    live_rows = jnp.arange(block_rows)[None, :] < counts_rows[:, None]

    def visit(position, maxima):
        return pair_update(
            unit_rows,
            rank_rows,
            live_rows,
            maxima,
            slot_pairs[position, 0],
            slot_pairs[position, 1],
        )

    start_maxima = jnp.zeros((unit_rows.shape[0], block_rows), jnp.float32)
    return lax.fori_loop(0, total_pairs, visit, start_maxima)


def local(embeddings, ranks, block_rows, pair_list, pair_count):
    held_blocks = embeddings.shape[0]
    own_units = normalize(embeddings)
    earlier = passed_along((own_units[1:], ranks[1:], block_rows[1:]), ("blk", "grp"), 1)
    window_units = jnp.concatenate([earlier[0], own_units], axis=0)
    window_ranks = jnp.concatenate([earlier[1], ranks], axis=0)
    window_counts = jnp.concatenate([earlier[2], block_rows], axis=0)
    maxima = run_pairs(window_units, window_ranks, window_counts, pair_list[0] - 1, pair_count[0])
    returned = passed_along(maxima[: held_blocks - 1], ("blk", "grp"), -1)
    widened = jnp.concatenate([jnp.zeros_like(returned[:1]), returned], axis=0)
    return jnp.maximum(maxima[held_blocks - 1 :], widened)


def solution(mesh):
    in_specs = (
        P(("blk", "grp"), None, None),
        P(("blk", "grp"), None),
        P(("blk", "grp")),
        P(("blk", "grp"), None, None),
        P(("blk", "grp")),
    )
    out_specs = P(("blk", "grp"), None)
    return jax.shard_map(local, mesh=mesh, in_specs=in_specs, out_specs=out_specs, check_vma=False)
```

profile of v0, /device:TPU:161, one launch (start us, length us, event | category | flops | bytes accessed | tf_op | source)
XLA Modules:
  0.0 201.9 jit_solution(3609055359682051333)
XLA Ops:
  0.0 0.0 copy-start.1
  0.0 4.2 %fusion.6 = f32[3,1024]{1,0:T(4,128)S(1)} fusion(bf16[3,1024,1024]{2,1,0:T(8,128)(2,1)} %param.11), kind=kLoop, calls=%fused_computation.24 | loop fusion | flops 9434112 | bytes 6303744 | tf_op jit(solution)/shard_map/reduce_sum | solution.py:15
  4.3 0.3 copy-done.1
  4.6 1.1 fusion.7
  5.7 0.0 copy-start
  5.7 2.6 %copy-done = bf16[3,1024,1024]{2,1,0:T(8,128)(2,1)} copy-done((bf16[3,1024,1024]{2,1,0:T(8,128)(2,1)}, bf16[3,1024,1024]{2,1,0:T(8,128)(2,1)S(1)}, u32[]{:S(2)}) %copy-start) | copy-done | bytes 6291480
  8.3 0.0 copy-start.2
  8.3 0.0 copy-start.5
  8.3 0.0 copy-start.4
  8.3 2.4 %slice.48 = bf16[2,1024,1024]{2,1,0:T(8,128)(2,1)} slice(bf16[3,1024,1024]{2,1,0:T(8,128)(2,1)S(1)} %fusion.7), slice={[1:3], [0:1024], [0:1024]} | slice | bytes 8388608 | tf_op jit(solution)/shard_map/slice | solution.py:56
  10.6 3.2 %collective-permute-start.2 = (bf16[2,1024,1024]{2,1,0:T(8,128)(2,1)}, bf16[2,1024,1024]{2,1,0:T(8,128)(2,1)}, u32[]{:S(2)}, u32[]{:S(2)}) collective-permute-start(bf16[2,1024,1024]{2,1,0:T(8,128)(2,1)} %slice.48), channel_id=1, source_target_pairs={{0,1},{1,2},{2,3},{3,4},{4,5},{5,6},{6,7},{7,8},{8,9},{9,10},{10,1... | collective-permute-start | bytes 12582920 | tf_op jit(solution)/shard_map/ppermute | solution.py:10
  13.8 0.0 copy-done.2
  13.9 3.2 %collective-permute-start.1 = (s32[2,1024]{1,0:T(2,128)S(1)}, s32[2,1024]{1,0:T(2,128)S(1)}, u32[]{:S(2)}, u32[]{:S(2)}) collective-permute-start(s32[2,1024]{1,0:T(2,128)S(1)} %slice.44), channel_id=1, source_target_pairs={{0,1},{1,2},{2,3},{3,4},{4,5},{5,6},{6,7},{7,8},{8,9},{9,10},{10,1... | collective-permute-start | bytes 24584 | tf_op jit(solution)/shard_map/ppermute | solution.py:10
  17.1 0.0 copy-done.5
  17.1 0.1 slice.43
  17.2 2.9 %collective-permute-start = (s32[2]{0:T(128)S(1)}, s32[2]{0:T(128)S(1)}, u32[]{:S(2)}, u32[]{:S(2)}) collective-permute-start(s32[2]{0:T(128)S(1)} %slice.43), channel_id=1, source_target_pairs={{0,1},{1,2},{2,3},{3,4},{4,5},{5,6},{6,7},{7,8},{8,9},{9,10},{10,1... | collective-permute-start | bytes 32 | tf_op jit(solution)/shard_map/ppermute | solution.py:10
  20.1 0.0 copy-done.4
  20.1 87.3 %collective-permute-done = s32[2]{0:T(128)S(1)} collective-permute-done((s32[2]{0:T(128)S(1)}, s32[2]{0:T(128)S(1)}, u32[]{:S(2)}, u32[]{:S(2)}) %collective-permute-start) | collective-permute-done | bytes 40 | tf_op jit(solution)/shard_map/ppermute | solution.py:10
  107.4 0.1 pad_add_fusion.3
  107.5 0.1 iota_compare_fusion
  107.6 0.0 collective-permute-done.1
  107.6 0.0 copy-start.3
  107.6 0.0 collective-permute-done.2
  107.6 9.7 %pad_maximum_fusion = bf16[5,1024,1024]{2,1,0:T(8,128)(2,1)} fusion(bf16[3,1024,1024]{2,1,0:T(8,128)(2,1)} %copy-done, bf16[2,1024,1024]{2,1,0:T(8,128)(2,1)} %collective-permute-done.2), kind=kLoop, calls=%fused_computation.26 | loop fusion | flops 5242880 | bytes 20971520 | tf_op jit(solution)/shard_map/concatenate | solution.py:57
  117.4 0.0 copy-done.3
  117.4 66.8 %while.12 = (s32[]{:T(128)}, f32[5,1024]{1,0:T(8,128)S(1)}, s32[]{:T(128)}, s32[6,2]{0,1:T(2,128)S(1)}, pred[5,1024]{1,0:T(8,128)(4,1)S(1)}, /*index=5*/s32[5,10...) while((s32[]{:T(128)}, f32[5,1024]{1,0:T(8,128)S(1)}, ...), condition=%wide.region_6.7_spmd, body=%wide.region_1.6_spmd.sunk | while | flops 2157971456 | bytes 4275503 | solution.py:50
  118.0 0.7 constant_dynamic-slice_fusion.6
  122.8 5.5 %select_reduce_fusion.3 = (f32[1024]{0:T(1024)S(1)}, f32[1024]{0:T(1024)S(1)}) fusion(s32[1024]{0:T(1024)S(1)} %bitcast.42, s32[1024]{0:T(1024)S(1)} %bitcast.41, pred[1024]{0:T(1024)(128)(4,1)S(1)} %get-tuple-element.151, pred[1024]{0:T(1024)(128)(4,1)S(1)} %get-tuple-element.152, bf16[5,1024,1024]{2,1,0:T(8,128)(2,1)} %get-tuple-element.188, ...), kind=kOutput, calls=%fused_computation.2.clone.1 | convolution fusion | flops 2157967360 | bytes 4213760 | tf_op jit(solution)/shard_map/while/body/dot_general | solution.py:22
  128.3 0.8 and_reduce_fusion.3
  129.0 0.6 broadcast_select_fusion.4
  129.7 0.1 scatter-max.12
  129.8 0.7 broadcast_select_fusion.5
  130.5 0.1 scatter-max.13
  131.3 0.7 constant_dynamic-slice_fusion.6
  136.0 5.5 %select_reduce_fusion.3 = (f32[1024]{0:T(1024)S(1)}, f32[1024]{0:T(1024)S(1)}) fusion(s32[1024]{0:T(1024)S(1)} %bitcast.42, s32[1024]{0:T(1024)S(1)} %bitcast.41, pred[1024]{0:T(1024)(128)(4,1)S(1)} %get-tuple-element.151, pred[1024]{0:T(1024)(128)(4,1)S(1)} %get-tuple-element.152, bf16[5,1024,1024]{2,1,0:T(8,128)(2,1)} %get-tuple-element.188, ...), kind=kOutput, calls=%fused_computation.2.clone.1 | convolution fusion | flops 2157967360 | bytes 4213760 | tf_op jit(solution)/shard_map/while/body/dot_general | solution.py:22
  141.5 0.8 and_reduce_fusion.3
  142.3 0.6 broadcast_select_fusion.4
  142.9 0.1 scatter-max.12
  143.0 0.7 broadcast_select_fusion.5
  143.7 0.1 scatter-max.13
  144.5 0.7 constant_dynamic-slice_fusion.6
  149.2 5.5 %select_reduce_fusion.3 = (f32[1024]{0:T(1024)S(1)}, f32[1024]{0:T(1024)S(1)}) fusion(s32[1024]{0:T(1024)S(1)} %bitcast.42, s32[1024]{0:T(1024)S(1)} %bitcast.41, pred[1024]{0:T(1024)(128)(4,1)S(1)} %get-tuple-element.151, pred[1024]{0:T(1024)(128)(4,1)S(1)} %get-tuple-element.152, bf16[5,1024,1024]{2,1,0:T(8,128)(2,1)} %get-tuple-element.188, ...), kind=kOutput, calls=%fused_computation.2.clone.1 | convolution fusion | flops 2157967360 | bytes 4213760 | tf_op jit(solution)/shard_map/while/body/dot_general | solution.py:22
  154.7 0.8 and_reduce_fusion.3
  155.5 0.6 broadcast_select_fusion.4
  156.1 0.1 scatter-max.12
  156.2 0.7 broadcast_select_fusion.5
  156.9 0.1 scatter-max.13
  157.7 0.7 constant_dynamic-slice_fusion.6
  162.5 5.5 %select_reduce_fusion.3 = (f32[1024]{0:T(1024)S(1)}, f32[1024]{0:T(1024)S(1)}) fusion(s32[1024]{0:T(1024)S(1)} %bitcast.42, s32[1024]{0:T(1024)S(1)} %bitcast.41, pred[1024]{0:T(1024)(128)(4,1)S(1)} %get-tuple-element.151, pred[1024]{0:T(1024)(128)(4,1)S(1)} %get-tuple-element.152, bf16[5,1024,1024]{2,1,0:T(8,128)(2,1)} %get-tuple-element.188, ...), kind=kOutput, calls=%fused_computation.2.clone.1 | convolution fusion | flops 2157967360 | bytes 4213760 | tf_op jit(solution)/shard_map/while/body/dot_general | solution.py:22
  167.9 0.8 and_reduce_fusion.3
  168.7 0.6 broadcast_select_fusion.4
  169.3 0.1 scatter-max.12
  169.4 0.7 broadcast_select_fusion.5
  170.1 0.1 scatter-max.13
  170.9 0.7 constant_dynamic-slice_fusion.6
  175.7 5.5 %select_reduce_fusion.3 = (f32[1024]{0:T(1024)S(1)}, f32[1024]{0:T(1024)S(1)}) fusion(s32[1024]{0:T(1024)S(1)} %bitcast.42, s32[1024]{0:T(1024)S(1)} %bitcast.41, pred[1024]{0:T(1024)(128)(4,1)S(1)} %get-tuple-element.151, pred[1024]{0:T(1024)(128)(4,1)S(1)} %get-tuple-element.152, bf16[5,1024,1024]{2,1,0:T(8,128)(2,1)} %get-tuple-element.188, ...), kind=kOutput, calls=%fused_computation.2.clone.1 | convolution fusion | flops 2157967360 | bytes 4213760 | tf_op jit(solution)/shard_map/while/body/dot_general | solution.py:22
  181.2 0.8 and_reduce_fusion.3
  182.0 0.6 broadcast_select_fusion.4
  182.6 0.1 scatter-max.12
  182.7 0.7 broadcast_select_fusion.5
  183.4 0.1 scatter-max.13
  184.2 16.3 %collective-permute-start.3 = (f32[2,1024]{1,0:T(2,128)S(1)}, f32[2,1024]{1,0:T(2,128)S(1)}, u32[]{:S(2)}, u32[]{:S(2)}) collective-permute-start(f32[2,1024]{1,0:T(2,128)S(1)} %slice.47), channel_id=1, source_target_pairs={{1,0},{2,1},{3,2},{4,3},{5,4},{6,5},{7,6},{8,7},{9,8},{10,9},{11,1... | collective-permute-start | bytes 24584 | tf_op jit(solution)/shard_map/ppermute | solution.py:10
  200.5 0.8 collective-permute-done.3
  201.3 0.6 pad_maximum_fusion.1
  (16 shorter events, 0.3 us)
Async XLA Ops:
  0.0 4.6 %copy-start.1 = (bf16[3,1024,1024]{2,1,0:T(8,128)(2,1)S(1)}, bf16[3,1024,1024]{2,1,0:T(8,128)(2,1)}, u32[]{:S(2)}) copy-start(bf16[3,1024,1024]{2,1,0:T(8,128)(2,1)} %param.11) | copy-start | bytes 18874372
  5.7 2.6 %copy-start = (bf16[3,1024,1024]{2,1,0:T(8,128)(2,1)}, bf16[3,1024,1024]{2,1,0:T(8,128)(2,1)S(1)}, u32[]{:S(2)}) copy-start(bf16[3,1024,1024]{2,1,0:T(8,128)(2,1)S(1)} %fusion.7) | copy-start | bytes 18874372
  8.3 5.6 %copy-start.2 = (s32[3,1024]{1,0:T(4,128)S(1)}, s32[3,1024]{1,0:T(4,128)}, u32[]{:S(2)}) copy-start(s32[3,1024]{1,0:T(4,128)} %param.12) | copy-start | bytes 36868
  8.3 8.8 %copy-start.5 = (s32[3]{0:T(128)S(1)}, s32[3]{0:T(128)}, u32[]{:S(2)}) copy-start(s32[3]{0:T(128)} %param.13) | copy-start | bytes 40
  8.3 11.8 %copy-start.4 = (s32[1,6,2]{1,2,0:T(2,128)S(1)}, s32[1,6,2]{1,2,0:T(2,128)}, u32[]{:S(2)}) copy-start(s32[1,6,2]{1,2,0:T(2,128)} %param.14) | copy-start | bytes 148
  10.6 97.0 %collective-permute-start.2 = (bf16[2,1024,1024]{2,1,0:T(8,128)(2,1)}, bf16[2,1024,1024]{2,1,0:T(8,128)(2,1)}, u32[]{:S(2)}, u32[]{:S(2)}) collective-permute-start(bf16[2,1024,1024]{2,1,0:T(8,128)(2,1)} %slice.48), channel_id=1, source_target_pairs={{0,1},{1,2},{2,3},{3,4},{4,5},{5,6},{6,7},{7,8},{8,9},{9,10},{10,1... | collective-permute-start | bytes 12582920 | tf_op jit(solution)/shard_map/ppermute | solution.py:10
  13.9 93.7 %collective-permute-start.1 = (s32[2,1024]{1,0:T(2,128)S(1)}, s32[2,1024]{1,0:T(2,128)S(1)}, u32[]{:S(2)}, u32[]{:S(2)}) collective-permute-start(s32[2,1024]{1,0:T(2,128)S(1)} %slice.44), channel_id=1, source_target_pairs={{0,1},{1,2},{2,3},{3,4},{4,5},{5,6},{6,7},{7,8},{8,9},{9,10},{10,1... | collective-permute-start | bytes 24584 | tf_op jit(solution)/shard_map/ppermute | solution.py:10
  17.2 90.2 %collective-permute-start = (s32[2]{0:T(128)S(1)}, s32[2]{0:T(128)S(1)}, u32[]{:S(2)}, u32[]{:S(2)}) collective-permute-start(s32[2]{0:T(128)S(1)} %slice.43), channel_id=1, source_target_pairs={{0,1},{1,2},{2,3},{3,4},{4,5},{5,6},{6,7},{7,8},{8,9},{9,10},{10,1... | collective-permute-start | bytes 32 | tf_op jit(solution)/shard_map/ppermute | solution.py:10
  107.6 9.8 %copy-start.3 = (s32[2]{0:T(128)S(1)}, s32[2]{0:T(128)}, u32[]{:S(2)}) copy-start(s32[2]{0:T(128)} %constant.59.clone.1) | copy-start | bytes 28
  184.2 17.1 %collective-permute-start.3 = (f32[2,1024]{1,0:T(2,128)S(1)}, f32[2,1024]{1,0:T(2,128)S(1)}, u32[]{:S(2)}, u32[]{:S(2)}) collective-permute-start(f32[2,1024]{1,0:T(2,128)S(1)} %slice.47), channel_id=1, source_target_pairs={{1,0},{2,1},{3,2},{4,3},{5,4},{6,5},{7,6},{8,7},{9,8},{10,9},{11,1... | collective-permute-start | bytes 24584 | tf_op jit(solution)/shard_map/ppermute | solution.py:10
where the time goes:
time: 205 us; the launch traced here: 202 us
  waiting for transfers between devices  88.1 us (43%)
  matrix products  27.4 us (13%)
  other arithmetic  26.2 us (13%)
  starting transfers between devices  25.6 us (12%)
  loops' own time  24.3 us (12%)
  local copies, waits for them, and re-layouts  10.1 us (5%)
    ppermute x4, waiting for transfers between devices, passed_along(): lax.ppermute(value, axis, [(source, source + steps) for source in range(l...  88.1 us
    dot_general x5, matrix products, pair_update(): lax.dot_general(left_rows, right_rows, (((1,), (1,)), ((), ())), preferre...  27.4 us
    ppermute x4, starting transfers between devices, passed_along(): lax.ppermute(value, axis, [(source, source + steps) for source in range(l...  25.6 us
    another operation x1, loops' own time, run_pairs(): return lax.fori_loop(0, total_pairs, visit, start_maxima)  24.3 us
    another operation x15, other arithmetic  10.4 us
    concatenate x1, other arithmetic, local(): window_units = jnp.concatenate([earlier[0], own_units], axis=0)  9.75 us
    reduce_sum x1, other arithmetic, normalize(): jnp.sum(values * values, axis=-1, keepdims=True) + 1e-06  4.24 us
  transfers between devices with their start and end apart: 4, of which 2 were waited for; matrix products, arithmetic and copies ran while one was open for 0% of the time, Pallas kernels for 0%

commit v1 on v0

v1 whole, which is shorter than its diff:
```python
import functools

import jax
import jax.numpy as jnp
from jax import lax
from jax.experimental import pallas as pl
from jax.experimental.pallas import tpu as pltpu
from jax.sharding import PartitionSpec as P

ROWS = 1024
DIM = 1024
HELD = 3
TILE = 256
LANES = 128
NONE = -1e30
DEAD = 1 << 30
AXES = ("blk", "grp")
CUTS = (0, 256, 768, 1024)


def passed_along(value, steps):
    count = lax.axis_size(AXES)
    leading, last = (max(0, -steps), min(count, count - steps))
    return lax.ppermute(value, AXES, [(source, source + steps) for source in range(leading, last)])


def unit_rows(raw):
    values = raw.astype(jnp.float32)
    scaling = lax.rsqrt(jnp.sum(values * values, axis=-1, keepdims=True) + 1e-06)
    return (values * scaling).astype(jnp.bfloat16)


def spread(keys_row):
    return jnp.broadcast_to(keys_row, (LANES, LANES)).T


def gathered(partial):
    return jnp.max(partial.T, axis=0, keepdims=True)


def pair_tile(left_units, left_keys, right_units, right_keys):
    similarity = lax.dot_general(
        left_units, right_units, (((1,), (1,)), ((), ())), preferred_element_type=jnp.float32
    )
    rows, cols = similarity.shape
    left_best = None
    right_best = []
    for group in range(cols // LANES):
        part = similarity[:, group * LANES : (group + 1) * LANES]
        keys = right_keys[:, group * LANES : (group + 1) * LANES]
        for_left = jnp.where(keys < left_keys, part, NONE)
        left_best = for_left if left_best is None else jnp.maximum(left_best, for_left)
        for_right = jnp.where(left_keys < keys, part, NONE)
        right_best.append(jnp.max(for_right.reshape(rows // 8, 8, LANES), axis=0))
    return left_best, jnp.concatenate(right_best, axis=1)


def local_kernel(pairs, count, raw, keys, units, best, spread_keys, left_acc, right_acc):
    for block in range(HELD):
        for group in range(ROWS // LANES):
            rows = pl.ds(group * LANES, LANES)
            spread_keys[block, rows, :] = spread(keys[block : block + 1, rows])

    def normalize(step, carry):
        block, rows = step // (ROWS // LANES), pl.ds((step % (ROWS // LANES)) * LANES, LANES)
        units[block, rows, :] = unit_rows(raw[block, rows, :])
        return carry

    lax.fori_loop(0, HELD * ROWS // LANES, normalize, 0)
    left_acc[...] = jnp.full_like(left_acc, NONE)
    right_acc[...] = jnp.full_like(right_acc, NONE)

    def visit(slot, carry):
        left, right = pairs[2 * slot], pairs[2 * slot + 1]

        @pl.when(right >= HELD)
        def _():
            def step(index, carry):
                rows = pl.ds((index // (ROWS // TILE)) * TILE, TILE)
                cols = pl.ds((index % (ROWS // TILE)) * TILE, TILE)
                left_best, right_best = pair_tile(
                    units[left - HELD, rows, :],
                    spread_keys[left - HELD, rows, :],
                    units[right - HELD, cols, :],
                    keys[pl.ds(right - HELD, 1), cols],
                )
                left_acc[left - HELD, rows, :] = jnp.maximum(left_acc[left - HELD, rows, :], left_best)
                right_acc[right - HELD, :, cols] = jnp.maximum(right_acc[right - HELD, :, cols], right_best)
                return carry

            lax.fori_loop(0, (ROWS // TILE) ** 2, step, 0)

        return carry

    lax.fori_loop(0, count[0], visit, 0)
    for block in range(HELD):
        for group in range(ROWS // LANES):
            rows = pl.ds(group * LANES, LANES)
            found = jnp.maximum(
                gathered(left_acc[block, rows, :]),
                jnp.max(right_acc[block, :, rows], axis=0, keepdims=True),
            )
            best[block : block + 1, rows] = jnp.maximum(1.0 + found, 0.0)


def local_pairs(pair_list, pair_count, embeddings, keys):
    smem, vmem = pl.BlockSpec(memory_space=pltpu.SMEM), pl.BlockSpec(memory_space=pltpu.VMEM)
    return pl.pallas_call(
        local_kernel,
        out_shape=(
            jax.ShapeDtypeStruct((HELD, ROWS, DIM), jnp.bfloat16),
            jax.ShapeDtypeStruct((HELD, ROWS), jnp.float32),
        ),
        in_specs=[smem, smem, vmem, vmem],
        out_specs=(vmem, vmem),
        scratch_shapes=[
            pltpu.VMEM((HELD, ROWS, LANES), jnp.int32),
            pltpu.VMEM((HELD, ROWS, LANES), jnp.float32),
            pltpu.VMEM((HELD, 8, ROWS), jnp.float32),
        ],
        compiler_params=pltpu.CompilerParams(vmem_limit_bytes=32 << 20),
        cost_estimate=pl.CostEstimate(flops=6 * 2 * ROWS * ROWS * DIM, bytes_accessed=4 * HELD * ROWS * DIM, transcendentals=0),
    )(pair_list.reshape(-1), pair_count, embeddings, keys)


def arrival_kernel(partners, flags, *refs):
    raws = refs[:-8]
    guest_keys, keys, units, guest_best, best, guest_units, left_acc, right_acc = refs[-8:]
    rows_in_all = sum(raw.shape[0] for raw in raws)
    left_acc[...] = jnp.full_like(left_acc, NONE)
    right_acc[...] = jnp.full_like(right_acc, NONE)

    @pl.when((flags[0] != 0) | (flags[1] != 0))
    def _():
        first = 0
        for raw in raws:
            def normalize(step, carry, raw=raw, first=first):
                start = pl.multiple_of(step * LANES, LANES)
                guest_units[pl.ds(first + start, LANES), :] = unit_rows(raw[pl.ds(start, LANES), :])
                return carry

            lax.fori_loop(0, raw.shape[0] // LANES, normalize, 0)
            first += raw.shape[0]

        for which, block in enumerate(partners):
            @pl.when(flags[which] != 0)
            def _(which=which, block=block):
                def step(index, carry):
                    start = pl.multiple_of((index // (ROWS // TILE)) * TILE, TILE)
                    rows, cols = pl.ds(start, TILE), pl.ds((index % (ROWS // TILE)) * TILE, TILE)
                    spread_keys = jnp.concatenate(
                        [spread(guest_keys[:, pl.ds(start + part * LANES, LANES)]) for part in range(TILE // LANES)], axis=0
                    )
                    left_best, right_best = pair_tile(
                        guest_units[rows, :], spread_keys, units[block, cols, :], keys[block : block + 1, cols]
                    )
                    left_acc[rows, :] = jnp.maximum(left_acc[rows, :], left_best)
                    right_acc[which, :, cols] = jnp.maximum(right_acc[which, :, cols], right_best)
                    return carry

                lax.fori_loop(0, rows_in_all // TILE * (ROWS // TILE), step, 0)

    for group in range(rows_in_all // LANES):
        rows = pl.ds(group * LANES, LANES)
        guest_best[:, rows] = jnp.maximum(1.0 + gathered(left_acc[rows, :]), 0.0)
    for which, block in enumerate(partners):
        found = jnp.max(right_acc[which], axis=0, keepdims=True)
        best[which : which + 1, :] = jnp.maximum(1.0 + found, 0.0)


def arrival_pairs(partners, flags, raws, guest_keys, keys, units):
    smem, vmem = pl.BlockSpec(memory_space=pltpu.SMEM), pl.BlockSpec(memory_space=pltpu.VMEM)
    rows = sum(raw.shape[0] for raw in raws)
    return pl.pallas_call(
        functools.partial(arrival_kernel, partners),
        out_shape=(
            jax.ShapeDtypeStruct((1, rows), jnp.float32),
            jax.ShapeDtypeStruct((2, ROWS), jnp.float32),
        ),
        in_specs=[smem] + [vmem] * (len(raws) + 3),
        out_specs=(vmem, vmem),
        scratch_shapes=[
            pltpu.VMEM((rows, DIM), jnp.bfloat16),
            pltpu.VMEM((rows, LANES), jnp.float32),
            pltpu.VMEM((2, 8, ROWS), jnp.float32),
        ],
        compiler_params=pltpu.CompilerParams(vmem_limit_bytes=32 << 20),
        cost_estimate=pl.CostEstimate(
            flops=2 * 2 * rows * ROWS * DIM, bytes_accessed=2 * (rows + HELD * ROWS) * DIM, transcendentals=0
        ),
    )(flags, *raws, guest_keys, keys, units)


def local(embeddings, ranks, block_rows, pair_list, pair_count):
    pieces = list(zip(CUTS[:-1], CUTS[1:]))
    keys = jnp.where(jnp.arange(ROWS)[None, :] < block_rows[:, None], ranks, DEAD)
    taken = jnp.arange(pair_list.shape[1]) < pair_count[0]
    listed = lambda u, v: jnp.any(taken & (pair_list[0, :, 0] == u) & (pair_list[0, :, 1] == v)).astype(jnp.int32)
    ahead = listed(HELD + 1, HELD - 1)
    left_flags = jnp.stack([ahead * listed(HELD, HELD - 1), ahead])
    sent_flags = jnp.stack([(1 - ahead) * listed(HELD, HELD - 1), listed(HELD, HELD - 2)])
    note = jnp.concatenate([keys[0], sent_flags, jnp.zeros((LANES - 2,), jnp.int32)])

    from_before, from_after = [], []
    for index, (low, high) in enumerate(pieces):
        if index == len(pieces) - 1:
            keys_before = passed_along(keys[HELD - 1], 1)
            note_after = passed_along(note, -1)
        from_before.append(passed_along(embeddings[HELD - 1, low:high], 1))
        from_after.append(passed_along(embeddings[0, low:high], -1))
    keys_before = keys_before[None, :]
    keys_after = note_after[None, :ROWS]
    right_flags = note_after[ROWS : ROWS + 2]

    units, best = local_pairs(pair_list, pair_count, embeddings, keys)

    split = CUTS[-2]
    before_early, best_before_early = arrival_pairs((0, 1), left_flags, from_before[:-1], keys_before[:, :split], keys, units)
    after_early, best_after_early = arrival_pairs((2, 1), right_flags, from_after[:-1], keys_after[:, :split], keys, units)
    before_late, best_before_late = arrival_pairs((0, 1), left_flags, from_before[-1:], keys_before[:, split:], keys, units)
    back = passed_along(jnp.concatenate([before_early, before_late], axis=1), -1)
    after_late, best_after_late = arrival_pairs((2, 1), right_flags, from_after[-1:], keys_after[:, split:], keys, units)
    onward = passed_along(jnp.concatenate([after_early, after_late], axis=1), 1)

    best_before = jnp.maximum(best_before_early, best_before_late)
    best_after = jnp.maximum(best_after_early, best_after_late)
    found = jnp.stack(
        [
            jnp.maximum(best_before[0], onward[0]),
            jnp.maximum(best_before[1], best_after[1]),
            jnp.maximum(best_after[0], back[0]),
        ]
    )
    return jnp.where(keys != DEAD, jnp.maximum(best, found), 0.0)


def solution(mesh):
    in_specs = (
        P(AXES, None, None),
        P(AXES, None),
        P(AXES),
        P(AXES, None, None),
        P(AXES),
    )
    return jax.shard_map(local, mesh=mesh, in_specs=in_specs, out_specs=P(AXES, None), check_vma=False)
```

time: 205 us -> 115 us (0.56)
  the two profiles are of different devices: /device:TPU:161 before, /device:TPU:224 now
where the time goes in v1:
time: 115 us; the launch traced here: 116 us
  starting transfers between devices  45.5 us (40%)
  Pallas kernels  42.5 us (37%)
  local copies, waits for them, and re-layouts  14.5 us (13%)
  waiting for transfers between devices  7.2 us (6%)
  between operations  3.45 us (3%)
  other arithmetic  3.08 us (3%)
    ppermute x10, starting transfers between devices, passed_along(): lax.ppermute(value, AXES, [(source, source + steps) for source in range(l...  45.5 us
    pallas_call x1, Pallas kernels, local_pairs(): pl.pallas_call(local_kernel, out_shape=(jax.ShapeDtypeStruct((HELD, ROWS,...  27 us
    pallas_call x4, Pallas kernels, arrival_pairs(): pl.pallas_call(functools.partial(arrival_kernel, partners), out_shape=(ja...  15.5 us
    unnamed x13, local copies, waits for them, and re-layouts  8.32 us
    ppermute x10, waiting for transfers between devices, passed_along(): lax.ppermute(value, AXES, [(source, source + steps) for source in range(l...  7.2 us
    squeeze x2, local copies, waits for them, and re-layouts, local(): from_after.append(passed_along(embeddings[0, low:high], -1))  6 us
  transfers between devices with their start and end apart: 10, of which 1 were waited for; matrix products, arithmetic and copies ran while one was open for 7% of the time, Pallas kernels for 37%

profile of v1, /device:TPU:224, one launch (start us, length us, event | category | flops | bytes accessed | tf_op | source)
XLA Modules:
  0.0 116.2 jit_solution(3018251970611026619)
XLA Ops:
  0.0 0.0 copy-start.4
  0.0 0.8 fusion.1.keys.refs_3_.refs_2_
  0.8 3.5 %collective-permute-start.2 = (s32[1024]{0:T(1024)S(1)}, s32[1024]{0:T(1024)S(1)}, u32[]{:S(2)}, u32[]{:S(2)}) collective-permute-start(s32[1024]{0:T(1024)S(1)} %bitcast.48), channel_id=1, source_target_pairs={{0,1},{1,2},{2,3},{3,4},{4,5},{5,6},{6,7},{7,8},{8,9},{9,10},{10,1... | collective-permute-start | bytes 12296 | tf_op jit(solution)/shard_map/ppermute | solution.py:24
  5.0 1.5 %fusion.2 = (pred[]{:T(512)}, pred[]{:T(512)}, pred[]{:T(512)}) fusion(s32[1,6,2]{1,2,0:T(2,128)} %param.8, s32[]{:T(128)} %bitcast.42), kind=kLoop, calls=%fused_computation.16 | loop fusion | flops 75 | bytes 55 | tf_op jit(solution)/shard_map/reduce_or | solution.py:198
  8.3 0.1 concatenate.9
  8.4 6.3 %collective-permute-start.4 = (s32[1152]{0:T(1024)S(1)}, s32[1152]{0:T(1024)S(1)}, u32[]{:S(2)}, u32[]{:S(2)}) collective-permute-start(s32[1152]{0:T(1024)S(1)} %concatenate.9), channel_id=1, source_target_pairs={{1,0},{2,1},{3,2},{4,3},{5,4},{6,5},{7,6},{8,7},{9,8},{10,9},{11,1... | collective-permute-start | bytes 13832 | tf_op jit(solution)/shard_map/ppermute | solution.py:24
  14.7 2.9 %slice_bitcast_fusion.2 = (bf16[256,1024]{1,0:T(8,128)(2,1)}, bf16[256,1024]{1,0:T(8,128)(2,1)}, bf16[256,1024]{1,0:T(8,128)(2,1)}, bf16[256,1024]{1,0:T(8,128)(2,1)}) fusion(bf16[3,1024,1024]{2,1,0:T(8,128)(2,1)} %raw.1), kind=kLoop, calls=%fused_computation.2 | loop fusion | bytes 4194304 | tf_op jit(solution)/shard_map/squeeze | solution.py:210
  17.6 2.5 %collective-permute-start.7 = (bf16[256,1024]{1,0:T(8,128)(2,1)}, bf16[256,1024]{1,0:T(8,128)(2,1)S(1)}, u32[]{:S(2)}, u32[]{:S(2)}) collective-permute-start(bf16[256,1024]{1,0:T(8,128)(2,1)} %get-tuple-element.28), channel_id=1, source_target_pairs={{1,0},{2,1},{3,2},{4,3},{5,4},{6,5},{7,6},{8,7},{9,8},{10,9},{11,1... | collective-permute-start | bytes 1572872 | tf_op jit(solution)/shard_map/ppermute | solution.py:24
  20.1 3.3 %collective-permute-start.3 = (bf16[256,1024]{1,0:T(8,128)(2,1)}, bf16[256,1024]{1,0:T(8,128)(2,1)S(1)}, u32[]{:S(2)}, u32[]{:S(2)}) collective-permute-start(bf16[256,1024]{1,0:T(8,128)(2,1)} %get-tuple-element.30), channel_id=1, source_target_pairs={{0,1},{1,2},{2,3},{3,4},{4,5},{5,6},{6,7},{7,8},{8,9},{9,10},{10,1... | collective-permute-start | bytes 1572872 | tf_op jit(solution)/shard_map/ppermute | solution.py:24
  23.5 1.9 %collective-permute-start = (bf16[256,1024]{1,0:T(8,128)(2,1)}, bf16[256,1024]{1,0:T(8,128)(2,1)}, u32[]{:S(2)}, u32[]{:S(2)}) collective-permute-start(bf16[256,1024]{1,0:T(8,128)(2,1)} %get-tuple-element.31), channel_id=1, source_target_pairs={{0,1},{1,2},{2,3},{3,4},{4,5},{5,6},{6,7},{7,8},{8,9},{9,10},{10,1... | collective-permute-start | bytes 1572872 | tf_op jit(solution)/shard_map/ppermute | solution.py:24
  25.4 3.1 %slice_bitcast_fusion = (bf16[512,1024]{1,0:T(8,128)(2,1)}, bf16[512,1024]{1,0:T(8,128)(2,1)}) fusion(bf16[3,1024,1024]{2,1,0:T(8,128)(2,1)} %raw.1), kind=kLoop, calls=%fused_computation | loop fusion | bytes 4194304 | tf_op jit(solution)/shard_map/squeeze | solution.py:210
  28.5 0.0 copy-done.4
  28.5 0.1 copy.7
  28.6 0.1 reshape.12.pairs
  28.6 0.0 collective-permute-done.2
  28.6 7.9 %collective-permute-start.6 = (bf16[512,1024]{1,0:T(8,128)(2,1)}, bf16[512,1024]{1,0:T(8,128)(2,1)S(1)}, u32[]{:S(2)}, u32[]{:S(2)}) collective-permute-start(bf16[512,1024]{1,0:T(8,128)(2,1)} %get-tuple-element.32), channel_id=1, source_target_pairs={{1,0},{2,1},{3,2},{4,3},{5,4},{6,5},{7,6},{8,7},{9,8},{10,9},{11,1... | collective-permute-start | bytes 3145736 | tf_op jit(solution)/shard_map/ppermute | solution.py:24
  36.5 0.0 collective-permute-done.4
  36.5 1.9 %collective-permute-start.1 = (bf16[512,1024]{1,0:T(8,128)(2,1)}, bf16[512,1024]{1,0:T(8,128)(2,1)S(1)}, u32[]{:S(2)}, u32[]{:S(2)}) collective-permute-start(bf16[512,1024]{1,0:T(8,128)(2,1)} %get-tuple-element.33), channel_id=1, source_target_pairs={{0,1},{1,2},{2,3},{3,4},{4,5},{5,6},{6,7},{7,8},{8,9},{9,10},{10,1... | collective-permute-start | bytes 3145736 | tf_op jit(solution)/shard_map/ppermute | solution.py:24
  38.4 0.0 copy-start.2
  38.5 2.8 %copy-done.2 = bf16[3,1024,1024]{2,1,0:T(8,128)(2,1)S(1)} copy-done((bf16[3,1024,1024]{2,1,0:T(8,128)(2,1)S(1)}, bf16[3,1024,1024]{2,1,0:T(8,128)(2,1)}, u32[]{:S(2)}) %copy-start.2) | copy-done | bytes 6291480
  41.2 27.0 %shard_map.55 = (bf16[3,1024,1024]{2,1,0:T(8,128)(2,1)S(1)}, f32[3,1024]{1,0:T(4,128)S(1)}) custom-call(s32[12]{0:T(128)S(1)} %reshape.12.pairs, s32[1]{0:T(128)} %copy.8.count, bf16[3,1024,1024]{2,1,0:T(8,128)(2,1)S(1)} %copy-done.2, s32[3,1024]{1,0:T(4,128)S(1)} %fusion.1.keys.refs_3_.refs_2_), custom_call_target="tpu_custom_call" | custom-call | flops 12884901888 | bytes 12582912 | tf_op jit(solution)/shard_map/pallas_call | solution.py:108
  68.2 0.0 copy-start
  68.3 2.7 %copy-done = bf16[3,1024,1024]{2,1,0:T(8,128)(2,1)} copy-done((bf16[3,1024,1024]{2,1,0:T(8,128)(2,1)}, bf16[3,1024,1024]{2,1,0:T(8,128)(2,1)S(1)}, u32[]{:S(2)}) %copy-start) | copy-done | bytes 6291480
  71.5 0.1 pad_add_fusion.flags
  71.6 0.0 collective-permute-done.3.refs_0_
  71.7 7.8 %collective-permute-start.5 = (bf16[256,1024]{1,0:T(8,128)(2,1)}, bf16[256,1024]{1,0:T(8,128)(2,1)S(1)}, u32[]{:S(2)}, u32[]{:S(2)}) collective-permute-start(bf16[256,1024]{1,0:T(8,128)(2,1)} %get-tuple-element.29), channel_id=1, source_target_pairs={{1,0},{2,1},{3,2},{4,3},{5,4},{6,5},{7,6},{8,7},{9,8},{10,9},{11,1... | collective-permute-start | bytes 1572872 | tf_op jit(solution)/shard_map/ppermute | solution.py:24
  79.5 0.0 copy-start.1
  79.5 2.8 %copy-done.1 = bf16[3,1024,1024]{2,1,0:T(8,128)(2,1)S(1)} copy-done((bf16[3,1024,1024]{2,1,0:T(8,128)(2,1)S(1)}, bf16[3,1024,1024]{2,1,0:T(8,128)(2,1)}, u32[]{:S(2)}) %copy-start.1) | copy-done | bytes 6291480
  82.3 0.7 shard_map.57
  83.0 0.0 collective-permute-done.7.refs_0_
  83.0 3.7 %shard_map.59 = (f32[1,256]{1,0:T(1,128)S(1)}, f32[2,1024]{1,0:T(2,128)S(1)}) custom-call(s32[2]{0:T(128)S(1)} %slice.91.flags, bf16[256,1024]{1,0:T(8,128)(2,1)S(1)} %collective-permute-done.7.refs_0_, s32[1,256]{1,0:T(1,128)S(1)} %slice.94.refs_1_, s32[3,1024]{1,0:T(4,128)S(1)} %fusion.1.keys.refs_3_.refs_2_, bf16[3,1024,1024]{2,1,0:T(8,128)(2,1)S(1)} %copy-done.1), custom_call_target="tpu_custom_call" | custom-call | flops 1073741824 | bytes 6815744 | tf_op jit(solution)/shard_map/pallas_call | solution.py:174
  86.7 0.0 collective-permute-done.refs_0_
  86.7 0.0 collective-permute-done.1.refs_1_
  86.7 1.3 %shard_map.56 = (f32[1,768]{1,0:T(1,128)S(1)}, f32[2,1024]{1,0:T(2,128)S(1)}) custom-call(s32[2]{0:T(128)S(1)} %pad_add_fusion.flags, bf16[256,1024]{1,0:T(8,128)(2,1)} %collective-permute-done.refs_0_, bf16[512,1024]{1,0:T(8,128)(2,1)S(1)} %collective-permute-done.1.refs_1_, s32[1,768]{1,0:T(1,128)S(1)} %slice.87.refs_2_, ...), custom_call_target="tpu_custom_call" | custom-call | flops 3221225472 | bytes 7864320 | tf_op jit(solution)/shard_map/pallas_call | solution.py:174
  88.0 0.0 copy-start.3
  88.0 0.0 copy-start.5
  88.0 8.4 %collective-permute-start.9 = (f32[1,1024]{1,0:T(1,128)S(1)}, f32[1,1024]{1,0:T(1,128)S(1)}, u32[]{:S(2)}, u32[]{:S(2)}) collective-permute-start(f32[1,1024]{1,0:T(1,128)S(1)} %pad_maximum_fusion.1), channel_id=1, source_target_pairs={{1,0},{2,1},{3,2},{4,3},{5,4},{6,5},{7,6},{8,7},{9,8},{10,9},{11,1... | collective-permute-start | bytes 12296 | tf_op jit(solution)/shard_map/ppermute | solution.py:24
  96.4 0.0 collective-permute-done.5.refs_0_
  96.4 0.0 collective-permute-done.6.refs_1_
  96.5 9.9 %shard_map.58 = (f32[1,768]{1,0:T(1,128)S(1)}, f32[2,1024]{1,0:T(2,128)S(1)}) custom-call(s32[2]{0:T(128)S(1)} %slice.91.flags, bf16[256,1024]{1,0:T(8,128)(2,1)S(1)} %collective-permute-done.5.refs_0_, bf16[512,1024]{1,0:T(8,128)(2,1)S(1)} %collective-permute-done.6.refs_1_, s32[1,768]{1,0:T(1,128)S(1)} %slice.93.refs_2_, ...), custom_call_target="tpu_custom_call" | custom-call | flops 3221225472 | bytes 7864320 | tf_op jit(solution)/shard_map/pallas_call | solution.py:174
  106.4 1.9 %collective-permute-start.8 = (f32[1,1024]{1,0:T(1,128)S(1)}, f32[1,1024]{1,0:T(1,128)S(1)}, u32[]{:S(2)}, u32[]{:S(2)}) collective-permute-start(f32[1,1024]{1,0:T(1,128)S(1)} %pad_maximum_fusion), channel_id=1, source_target_pairs={{0,1},{1,2},{2,3},{3,4},{4,5},{5,6},{6,7},{7,8},{8,9},{9,10},{10,1... | collective-permute-start | bytes 12296 | tf_op jit(solution)/shard_map/ppermute | solution.py:24
  108.3 0.0 collective-permute-done.9
  108.3 7.2 %collective-permute-done.8 = f32[1,1024]{1,0:T(1,128)S(1)} collective-permute-done((f32[1,1024]{1,0:T(1,128)S(1)}, f32[1,1024]{1,0:T(1,128)S(1)}, u32[]{:S(2)}, u32[]{:S(2)}) %collective-permute-start.8) | collective-permute-done | bytes 4128 | tf_op jit(solution)/shard_map/ppermute | solution.py:24
  115.5 0.0 copy-done.3
  115.5 0.0 copy-done.5
  115.5 0.7 fusion
  (13 shorter events, 0.1 us)
Async XLA Ops:
  0.0 28.5 %copy-start.4 = (s32[1,6,2]{1,2,0:T(2,128)S(1)}, s32[1,6,2]{1,2,0:T(2,128)}, u32[]{:S(2)}) copy-start(s32[1,6,2]{1,2,0:T(2,128)} %param.8) | copy-start | bytes 148
  0.8 27.8 %collective-permute-start.2 = (s32[1024]{0:T(1024)S(1)}, s32[1024]{0:T(1024)S(1)}, u32[]{:S(2)}, u32[]{:S(2)}) collective-permute-start(s32[1024]{0:T(1024)S(1)} %bitcast.48), channel_id=1, source_target_pairs={{0,1},{1,2},{2,3},{3,4},{4,5},{5,6},{6,7},{7,8},{8,9},{9,10},{10,1... | collective-permute-start | bytes 12296 | tf_op jit(solution)/shard_map/ppermute | solution.py:24
  8.4 28.1 %collective-permute-start.4 = (s32[1152]{0:T(1024)S(1)}, s32[1152]{0:T(1024)S(1)}, u32[]{:S(2)}, u32[]{:S(2)}) collective-permute-start(s32[1152]{0:T(1024)S(1)} %concatenate.9), channel_id=1, source_target_pairs={{1,0},{2,1},{3,2},{4,3},{5,4},{6,5},{7,6},{8,7},{9,8},{10,9},{11,1... | collective-permute-start | bytes 13832 | tf_op jit(solution)/shard_map/ppermute | solution.py:24
  17.6 65.3 %collective-permute-start.7 = (bf16[256,1024]{1,0:T(8,128)(2,1)}, bf16[256,1024]{1,0:T(8,128)(2,1)S(1)}, u32[]{:S(2)}, u32[]{:S(2)}) collective-permute-start(bf16[256,1024]{1,0:T(8,128)(2,1)} %get-tuple-element.28), channel_id=1, source_target_pairs={{1,0},{2,1},{3,2},{4,3},{5,4},{6,5},{7,6},{8,7},{9,8},{10,9},{11,1... | collective-permute-start | bytes 1572872 | tf_op jit(solution)/shard_map/ppermute | solution.py:24
  20.1 51.5 %collective-permute-start.3 = (bf16[256,1024]{1,0:T(8,128)(2,1)}, bf16[256,1024]{1,0:T(8,128)(2,1)S(1)}, u32[]{:S(2)}, u32[]{:S(2)}) collective-permute-start(bf16[256,1024]{1,0:T(8,128)(2,1)} %get-tuple-element.30), channel_id=1, source_target_pairs={{0,1},{1,2},{2,3},{3,4},{4,5},{5,6},{6,7},{7,8},{8,9},{9,10},{10,1... | collective-permute-start | bytes 1572872 | tf_op jit(solution)/shard_map/ppermute | solution.py:24
  23.5 63.2 %collective-permute-start = (bf16[256,1024]{1,0:T(8,128)(2,1)}, bf16[256,1024]{1,0:T(8,128)(2,1)}, u32[]{:S(2)}, u32[]{:S(2)}) collective-permute-start(bf16[256,1024]{1,0:T(8,128)(2,1)} %get-tuple-element.31), channel_id=1, source_target_pairs={{0,1},{1,2},{2,3},{3,4},{4,5},{5,6},{6,7},{7,8},{8,9},{9,10},{10,1... | collective-permute-start | bytes 1572872 | tf_op jit(solution)/shard_map/ppermute | solution.py:24
  28.6 67.8 %collective-permute-start.6 = (bf16[512,1024]{1,0:T(8,128)(2,1)}, bf16[512,1024]{1,0:T(8,128)(2,1)S(1)}, u32[]{:S(2)}, u32[]{:S(2)}) collective-permute-start(bf16[512,1024]{1,0:T(8,128)(2,1)} %get-tuple-element.32), channel_id=1, source_target_pairs={{1,0},{2,1},{3,2},{4,3},{5,4},{6,5},{7,6},{8,7},{9,8},{10,9},{11,1... | collective-permute-start | bytes 3145736 | tf_op jit(solution)/shard_map/ppermute | solution.py:24
  36.5 50.2 %collective-permute-start.1 = (bf16[512,1024]{1,0:T(8,128)(2,1)}, bf16[512,1024]{1,0:T(8,128)(2,1)S(1)}, u32[]{:S(2)}, u32[]{:S(2)}) collective-permute-start(bf16[512,1024]{1,0:T(8,128)(2,1)} %get-tuple-element.33), channel_id=1, source_target_pairs={{0,1},{1,2},{2,3},{3,4},{4,5},{5,6},{6,7},{7,8},{8,9},{9,10},{10,1... | collective-permute-start | bytes 3145736 | tf_op jit(solution)/shard_map/ppermute | solution.py:24
  38.4 2.8 %copy-start.2 = (bf16[3,1024,1024]{2,1,0:T(8,128)(2,1)S(1)}, bf16[3,1024,1024]{2,1,0:T(8,128)(2,1)}, u32[]{:S(2)}) copy-start(bf16[3,1024,1024]{2,1,0:T(8,128)(2,1)} %raw.1) | copy-start | bytes 18874372
  68.2 2.7 %copy-start = (bf16[3,1024,1024]{2,1,0:T(8,128)(2,1)}, bf16[3,1024,1024]{2,1,0:T(8,128)(2,1)S(1)}, u32[]{:S(2)}) copy-start(bf16[3,1024,1024]{2,1,0:T(8,128)(2,1)S(1)} %get-tuple-element.16.refs_4_.refs_3_) | copy-start | bytes 18874372
  71.7 24.8 %collective-permute-start.5 = (bf16[256,1024]{1,0:T(8,128)(2,1)}, bf16[256,1024]{1,0:T(8,128)(2,1)S(1)}, u32[]{:S(2)}, u32[]{:S(2)}) collective-permute-start(bf16[256,1024]{1,0:T(8,128)(2,1)} %get-tuple-element.29), channel_id=1, source_target_pairs={{1,0},{2,1},{3,2},{4,3},{5,4},{6,5},{7,6},{8,7},{9,8},{10,9},{11,1... | collective-permute-start | bytes 1572872 | tf_op jit(solution)/shard_map/ppermute | solution.py:24
  79.5 2.8 %copy-start.1 = (bf16[3,1024,1024]{2,1,0:T(8,128)(2,1)S(1)}, bf16[3,1024,1024]{2,1,0:T(8,128)(2,1)}, u32[]{:S(2)}) copy-start(bf16[3,1024,1024]{2,1,0:T(8,128)(2,1)} %copy-done) | copy-start | bytes 18874372
  88.0 27.5 %copy-start.3 = (s32[3,1024]{1,0:T(4,128)S(1)}, s32[3,1024]{1,0:T(4,128)}, u32[]{:S(2)}) copy-start(s32[3,1024]{1,0:T(4,128)} %param.6) | copy-start | bytes 36868
  88.0 27.5 %copy-start.5 = (s32[3]{0:T(128)S(1)}, s32[3]{0:T(128)}, u32[]{:S(2)}) copy-start(s32[3]{0:T(128)} %param.7) | copy-start | bytes 40
  88.0 20.3 %collective-permute-start.9 = (f32[1,1024]{1,0:T(1,128)S(1)}, f32[1,1024]{1,0:T(1,128)S(1)}, u32[]{:S(2)}, u32[]{:S(2)}) collective-permute-start(f32[1,1024]{1,0:T(1,128)S(1)} %pad_maximum_fusion.1), channel_id=1, source_target_pairs={{1,0},{2,1},{3,2},{4,3},{5,4},{6,5},{7,6},{8,7},{9,8},{10,9},{11,1... | collective-permute-start | bytes 12296 | tf_op jit(solution)/shard_map/ppermute | solution.py:24
  106.4 9.1 %collective-permute-start.8 = (f32[1,1024]{1,0:T(1,128)S(1)}, f32[1,1024]{1,0:T(1,128)S(1)}, u32[]{:S(2)}, u32[]{:S(2)}) collective-permute-start(f32[1,1024]{1,0:T(1,128)S(1)} %pad_maximum_fusion), channel_id=1, source_target_pairs={{0,1},{1,2},{2,3},{3,4},{4,5},{5,6},{6,7},{7,8},{8,9},{9,10},{10,1... | collective-permute-start | bytes 12296 | tf_op jit(solution)/shard_map/ppermute | solution.py:24

commit v2 on v1

v2 whole, which is shorter than its diff:
```python
import functools

import jax
import jax.numpy as jnp
from jax import lax
from jax.experimental import pallas as pl
from jax.experimental.pallas import tpu as pltpu
from jax.sharding import PartitionSpec as P

ROWS = 1024
DIM = 1024
HELD = 3
COLS = 256
LANES = 128
NOTE = 16
EARLY = 768
LATE = ROWS - EARLY
DIGIT = 128
DEAD = DIGIT**3 - 1
NONE = -1e30
AXES = ("blk", "grp")
SMEM = pl.BlockSpec(memory_space=pltpu.SMEM)
VMEM = pl.BlockSpec(memory_space=pltpu.VMEM)
HBM = pl.BlockSpec(memory_space=pltpu.HBM)


def passed_along(value, steps):
    count = lax.axis_size(AXES)
    leading, last = (max(0, -steps), min(count, count - steps))
    return lax.ppermute(value, AXES, [(source, source + steps) for source in range(leading, last)])


def shaped(shape, dtype):
    return jax.ShapeDtypeStruct(shape, dtype)


def unit_rows(raw):
    values = raw.astype(jnp.float32)
    scaling = lax.rsqrt(jnp.sum(values * values, axis=-1, keepdims=True) + 1e-06)
    return (values * scaling).astype(jnp.bfloat16)


def normalize(raw, units, rows):
    def step(index, carry):
        at = pl.ds(pl.multiple_of(index * LANES, LANES), LANES)
        units[at, :] = unit_rows(raw[at, :])
        return carry

    lax.fori_loop(0, rows // LANES, step, 0, unroll=2)


def spread(keys_row):
    return jnp.broadcast_to(keys_row, (LANES, LANES)).T


def gathered(partial):
    return jnp.max(partial.T, axis=0, keepdims=True)


def shifted(found):
    return jnp.maximum(1.0 + found, 0.0)


def pair_tile(left_units, left_keys, right_units, right_keys):
    similarity = lax.dot_general(
        left_units, right_units, (((1,), (1,)), ((), ())), preferred_element_type=jnp.float32
    )
    rows, cols = similarity.shape
    left_best = None
    right_best = []
    for group in range(cols // LANES):
        part = similarity[:, group * LANES : (group + 1) * LANES]
        keys = right_keys[:, group * LANES : (group + 1) * LANES]
        for_left = jnp.where(keys < left_keys, part, NONE)
        left_best = for_left if left_best is None else jnp.maximum(left_best, for_left)
        for_right = jnp.where(left_keys < keys, part, NONE)
        right_best.append(jnp.max(for_right.reshape(rows // 8, 8, LANES), axis=0))
    return left_best, jnp.concatenate(right_best, axis=1)


def pair_strip(first, left_units, left_keys, left_acc, right_units, right_keys, right_acc, cols):
    rows = pl.ds(first, left_units.shape[0] - first)
    left_best, right_best = pair_tile(left_units[rows, :], left_keys[rows, :], right_units[cols, :], right_keys[:, cols])
    left_acc[rows, :] = jnp.maximum(left_acc[rows, :], left_best)
    right_acc[:, cols] = jnp.maximum(right_acc[:, cols], right_best)


def note_rows(keys, flags):
    row = lax.broadcasted_iota(jnp.int32, (NOTE, ROWS), 0)
    values = [keys % DIGIT, (keys // DIGIT) % DIGIT, keys // DIGIT**2] + flags
    note = jnp.zeros((NOTE, ROWS), jnp.int32)
    for index, value in enumerate(values):
        note = jnp.where(row == index, value, note)
    return note.astype(jnp.float32).astype(jnp.bfloat16)


def noted_keys(note):
    digits = note.astype(jnp.float32).astype(jnp.int32)
    return digits[0:1] + digits[1:2] * DIGIT + digits[2:3] * DIGIT**2


def early_kernel(pairs, count, live, ranks, raw, onward, back, keys, flags, sems):
    copies = [
        pltpu.make_async_copy(raw.at[block, pl.ds(0, EARLY)], piece.at[pl.ds(0, EARLY)], sems.at[index])
        for index, (block, piece) in enumerate(((HELD - 1, onward), (0, back)))
    ]
    for copy in copies:
        copy.start()
    position = lax.broadcasted_iota(jnp.int32, (1, ROWS), 1)
    for block in range(HELD):
        keys[block : block + 1, :] = jnp.where(position < live[block], ranks[block : block + 1, :], DEAD)

    def listed(u, v):
        found = jnp.int32(0)
        for slot in range(pairs.shape[2]):
            hit = (slot < count[0]) & (pairs[0, 0, slot] == u) & (pairs[0, 1, slot] == v)
            found = found | hit.astype(jnp.int32)
        return found

    ahead, near, far = listed(HELD + 1, HELD - 1), listed(HELD, HELD - 1), listed(HELD, HELD - 2)
    flags[0] = ahead * near
    flags[1] = ahead
    onward[pl.ds(EARLY, NOTE), :] = note_rows(keys[HELD - 1 : HELD, :], [])
    back[pl.ds(EARLY, NOTE), :] = note_rows(keys[0:1, :], [(1 - ahead) * near, far])
    for copy in copies:
        copy.wait()


def early_pieces(pairs, count, live, ranks, raw):
    piece = shaped((EARLY + NOTE, DIM), jnp.bfloat16)
    return pl.pallas_call(
        early_kernel,
        out_shape=(piece, piece, shaped((HELD, ROWS), jnp.int32), shaped((2,), jnp.int32)),
        in_specs=[SMEM, SMEM, SMEM, VMEM, HBM],
        out_specs=(VMEM, VMEM, VMEM, SMEM),
        scratch_shapes=[pltpu.SemaphoreType.DMA((2,))],
        compiler_params=pltpu.CompilerParams(vmem_limit_bytes=6 << 20),
        cost_estimate=pl.CostEstimate(flops=0, bytes_accessed=8 * EARLY * DIM, transcendentals=0),
    )(pairs, count, live, ranks, raw)


def late_kernel(flags, raw, onward, back, flags_again, sems):
    copies = [
        pltpu.make_async_copy(raw.at[block, pl.ds(EARLY, LATE)], piece, sems.at[index])
        for index, (block, piece) in enumerate(((HELD - 1, onward), (0, back)))
    ]
    for copy in copies:
        copy.start()
    flags_again[0] = flags[0]
    flags_again[1] = flags[1]
    for copy in copies:
        copy.wait()


def late_pieces(flags, raw):
    piece = shaped((LATE, DIM), jnp.bfloat16)
    return pl.pallas_call(
        late_kernel,
        out_shape=(piece, piece, shaped((2,), jnp.int32)),
        in_specs=[SMEM, HBM],
        out_specs=(VMEM, VMEM, SMEM),
        scratch_shapes=[pltpu.SemaphoreType.DMA((2,))],
        compiler_params=pltpu.CompilerParams(vmem_limit_bytes=4 << 20),
        cost_estimate=pl.CostEstimate(flops=0, bytes_accessed=8 * LATE * DIM, transcendentals=0),
    )(flags, raw)


def local_kernel(pairs, count, flags, raw, keys, units, best, spread_keys, left_acc, right_acc):
    for block in range(HELD):
        for group in range(ROWS // LANES):
            rows = pl.ds(group * LANES, LANES)
            spread_keys[block, rows, :] = spread(keys[block : block + 1, rows])
        normalize(raw.at[block], units.at[block], ROWS)
    left_acc[...] = jnp.full_like(left_acc, NONE)
    right_acc[...] = jnp.full_like(right_acc, NONE)

    def visit(slot, carry):
        left, right = pairs[0, 0, slot] - HELD, pairs[0, 1, slot] - HELD

        def strip(first, col):
            pair_strip(
                first, units.at[left], spread_keys.at[left], left_acc.at[left],
                units.at[right], keys.at[pl.ds(right, 1)], right_acc.at[right], pl.ds(col, COLS),
            )

        @pl.when(right == left)
        def _():
            for col in range(0, ROWS, COLS):
                strip(col, col)

        @pl.when((right >= 0) & (right != left))
        def _():
            for col in range(0, ROWS, COLS):
                strip(0, col)

        return carry

    lax.fori_loop(0, count[0], visit, 0)
    for block in range(HELD):
        for group in range(ROWS // LANES):
            rows = pl.ds(group * LANES, LANES)
            found = jnp.maximum(
                gathered(left_acc[block, rows, :]),
                jnp.max(right_acc[block, :, rows], axis=0, keepdims=True),
            )
            best[block : block + 1, rows] = shifted(found)


def local_pairs(pairs, count, flags, raw, keys):
    return pl.pallas_call(
        local_kernel,
        out_shape=(shaped((HELD, ROWS, DIM), jnp.bfloat16), shaped((HELD, ROWS), jnp.float32)),
        in_specs=[SMEM, SMEM, SMEM, VMEM, VMEM],
        out_specs=(VMEM, VMEM),
        scratch_shapes=[
            pltpu.VMEM((HELD, ROWS, LANES), jnp.int32),
            pltpu.VMEM((HELD, ROWS, LANES), jnp.float32),
            pltpu.VMEM((HELD, 8, ROWS), jnp.float32),
        ],
        compiler_params=pltpu.CompilerParams(vmem_limit_bytes=24 << 20),
        cost_estimate=pl.CostEstimate(flops=6 * 2 * ROWS * ROWS * DIM, bytes_accessed=4 * HELD * ROWS * DIM, transcendentals=0),
    )(pairs, count, flags, raw, keys)


def guest_pairs(flags, block_of, guest_rows, raw, guest_keys, keys, units, guest_units, spread_keys, left_acc, right_acc):
    left_acc[...] = jnp.full_like(left_acc, NONE)

    @pl.when((flags[0] != 0) | (flags[1] != 0))
    def _():
        normalize(raw, guest_units, guest_rows)
        for group in range(guest_rows // LANES):
            rows = pl.ds(group * LANES, LANES)
            spread_keys[rows, :] = spread(guest_keys[:, group * LANES : (group + 1) * LANES])

        def visit(which, carry):
            block = block_of(which)

            @pl.when(flags[which] != 0)
            def _():
                for col in range(0, ROWS, COLS):
                    pair_strip(
                        0, guest_units, spread_keys, left_acc,
                        units.at[block], keys.at[pl.ds(block, 1)], right_acc.at[block], pl.ds(col, COLS),
                    )

            return carry

        lax.fori_loop(0, 2, visit, 0)


def finish(left_acc, guest_best, first, right_acc, best_before, best):
    for group in range(left_acc.shape[0] // LANES):
        rows = pl.ds(group * LANES, LANES)
        guest_best[:, pl.ds(first + group * LANES, LANES)] = shifted(gathered(left_acc[rows, :]))
    if best is not None:
        for block in range(HELD):
            found = jnp.max(right_acc[block], axis=0, keepdims=True)
            best[block : block + 1, :] = jnp.maximum(best_before[block : block + 1, :], shifted(found))


def from_before(which):
    return which


def from_after(which):
    return HELD - 1 - which


def middle_kernel(
    flags, raw_before, raw_after, keys, units, best_before,
    guest_before, guest_after, best, keys_before, keys_after, flags_after,
    guest_units, spread_keys, left_acc, right_acc,
):
    keys_before[...] = noted_keys(raw_before[pl.ds(EARLY, NOTE), :])
    note = raw_after[pl.ds(EARLY, NOTE), :]
    keys_after[...] = noted_keys(note)
    for which in range(2):
        flags_after[which] = (jnp.max(note[3 + which : 4 + which, :].astype(jnp.float32)) > 0.5).astype(jnp.int32)
    right_acc[...] = jnp.full_like(right_acc, NONE)
    common = (keys, units, guest_units, spread_keys, left_acc, right_acc)
    guest_pairs(flags, from_before, EARLY, raw_before, keys_before[:, :EARLY], *common)
    finish(left_acc, guest_before, 0, right_acc, None, None)
    guest_pairs(flags_after, from_after, EARLY, raw_after, keys_after[:, :EARLY], *common)
    finish(left_acc, guest_after, 0, right_acc, best_before, best)


def guest_scratch(rows):
    return [
        pltpu.VMEM((rows, DIM), jnp.bfloat16),
        pltpu.VMEM((rows, LANES), jnp.int32),
        pltpu.VMEM((rows, LANES), jnp.float32),
        pltpu.VMEM((HELD, 8, ROWS), jnp.float32),
    ]


def middle_pairs(flags, raw_before, raw_after, keys, units, best_before):
    row = shaped((1, ROWS), jnp.int32)
    guest = shaped((1, EARLY), jnp.float32)
    return pl.pallas_call(
        middle_kernel,
        out_shape=(guest, guest, shaped((HELD, ROWS), jnp.float32), row, row, shaped((2,), jnp.int32)),
        in_specs=[SMEM] + [VMEM] * 5,
        out_specs=(VMEM,) * 5 + (SMEM,),
        scratch_shapes=guest_scratch(EARLY),
        compiler_params=pltpu.CompilerParams(vmem_limit_bytes=18 << 20),
        cost_estimate=pl.CostEstimate(flops=6 * EARLY * ROWS * DIM, bytes_accessed=2 * (2 * EARLY + HELD * ROWS) * DIM, transcendentals=0),
    )(flags, raw_before, raw_after, keys, units, best_before)


def last_kernel(
    block_of, flags, raw, guest_keys, keys, units, guest_early, best_before, guest_best, best,
    guest_units, spread_keys, left_acc, right_acc,
):
    right_acc[...] = jnp.full_like(right_acc, NONE)
    guest_pairs(flags, block_of, LATE, raw, guest_keys[:, EARLY:], keys, units, guest_units, spread_keys, left_acc, right_acc)
    guest_best[:, pl.ds(0, EARLY)] = guest_early[...]
    finish(left_acc, guest_best, EARLY, right_acc, best_before, best)


def last_pairs(block_of, flags, raw, guest_keys, keys, units, guest_early, best_before):
    return pl.pallas_call(
        functools.partial(last_kernel, block_of),
        out_shape=(shaped((1, ROWS), jnp.float32), shaped((HELD, ROWS), jnp.float32)),
        in_specs=[SMEM] + [VMEM] * 6,
        out_specs=(VMEM, VMEM),
        scratch_shapes=guest_scratch(LATE),
        compiler_params=pltpu.CompilerParams(vmem_limit_bytes=12 << 20),
        cost_estimate=pl.CostEstimate(flops=4 * LATE * ROWS * DIM, bytes_accessed=2 * (LATE + HELD * ROWS) * DIM, transcendentals=0),
    )(flags, raw, guest_keys, keys, units, guest_early, best_before)


def local(embeddings, ranks, block_rows, pair_list, pair_count):
    pairs = pair_list.transpose(0, 2, 1)
    early_on, early_back, keys, flags = early_pieces(pairs, pair_count, block_rows, ranks, embeddings)
    late_on, late_back, flags = late_pieces(flags, embeddings)
    early_before, early_after = passed_along(early_on, 1), passed_along(early_back, -1)
    late_before, late_after = passed_along(late_on, 1), passed_along(late_back, -1)
    units, best = local_pairs(pairs, pair_count, flags, embeddings, keys)
    guest_before, guest_after, best, keys_before, keys_after, flags_after = middle_pairs(
        flags, early_before, early_after, keys, units, best
    )
    returned, best = last_pairs(from_before, flags, late_before, keys_before, keys, units, guest_before, best)
    back = passed_along(returned, -1)
    returned, best = last_pairs(from_after, flags_after, late_after, keys_after, keys, units, guest_after, best)
    onward = passed_along(returned, 1)
    found = jnp.concatenate([onward, jnp.zeros_like(onward), back], axis=0)
    return jnp.where(keys != DEAD, jnp.maximum(best, found), 0.0)


def solution(mesh):
    in_specs = (
        P(AXES, None, None),
        P(AXES, None),
        P(AXES),
        P(AXES, None, None),
        P(AXES),
    )
    return jax.shard_map(local, mesh=mesh, in_specs=in_specs, out_specs=P(AXES, None), check_vma=False)
```

time: 115 us -> 82.3 us (0.72)
  the two profiles are of different devices: /device:TPU:224 before, /device:TPU:161 now
where the time goes in v2:
time: 82.3 us
  starting transfers between devices  25.7 us (31%)
  waiting for transfers between devices  25.7 us (31%)
  Pallas kernels  24.6 us (30%)
  local copies, waits for them, and re-layouts  4.91 us (6%)
    ppermute x6, waiting for transfers between devices, passed_along(): lax.ppermute(value, AXES, [(source, source + steps) for source in range(l...  25.7 us
    ppermute x6, starting transfers between devices, passed_along(): lax.ppermute(value, AXES, [(source, source + steps) for source in range(l...  25.7 us
    pallas_call x1, Pallas kernels, local_pairs(): pl.pallas_call(local_kernel, out_shape=(shaped((HELD, ROWS, DIM), jnp.bfl...  11.8 us
    pallas_call x1, Pallas kernels, middle_pairs(): pl.pallas_call(middle_kernel, out_shape=(guest, guest, shaped((HELD, ROWS...  6.73 us
    unnamed x12, local copies, waits for them, and re-layouts  4.84 us
    pallas_call x2, Pallas kernels, last_pairs(): pl.pallas_call(functools.partial(last_kernel, block_of), out_shape=(shape...  3.38 us
  transfers between devices with their start and end apart: 6, of which 3 were waited for; matrix products, arithmetic and copies ran while one was open for 0% of the time, Pallas kernels for 28%

profile of v2, /device:TPU:161, one launch (start us, length us, event | category | flops | bytes accessed | tf_op | source)
XLA Modules:
  0.0 82.3 jit_solution(82006891979961596)
XLA Ops:
  0.7 0.0 copy-start
  0.7 2.8 %copy-done = bf16[3,1024,1024]{2,1,0:T(8,128)(2,1)S(1)} copy-done((bf16[3,1024,1024]{2,1,0:T(8,128)(2,1)S(1)}, bf16[3,1024,1024]{2,1,0:T(8,128)(2,1)}, u32[]{:S(2)}) %copy-start) | copy-done | bytes 6291480
  3.4 0.0 copy-start.2
  3.4 0.7 copy-done.2
  4.2 0.0 copy-start.3
  4.2 0.7 copy-done.3
  4.8 0.0 copy-start.5
  4.8 0.7 copy-done.5
  5.5 0.0 copy-start.1
  5.5 1.4 %shard_map.55 = (bf16[784,1024]{1,0:T(8,128)(2,1)S(1)}, bf16[784,1024]{1,0:T(8,128)(2,1)S(1)}, s32[3,1024]{1,0:T(4,128)S(1)}, s32[2]{0:T(128)S(1)}) custom-call(s32[1,2,6]{2,1,0:T(2,128)S(1)} %bitcast.2, s32[1]{0:T(128)S(6)} %copy.6.count, s32[3]{0:T(128)S(1)} %copy-done.5, s32[3,1024]{1,0:T(4,128)S(1)} %copy-done.2, bf16[3,1024,1024]{2,1,0:T(8,128)(2,1)S(1)} %copy-done), custom_call_target="tpu_custom_call" | custom-call | bytes 6291456 | tf_op jit(solution)/shard_map/pallas_call | solution.py:131
  6.9 3.3 %collective-permute-start = (bf16[784,1024]{1,0:T(8,128)(2,1)S(1)}, bf16[784,1024]{1,0:T(8,128)(2,1)S(1)}, u32[]{:S(2)}, u32[]{:S(2)}) collective-permute-start(bf16[784,1024]{1,0:T(8,128)(2,1)S(1)} %get-tuple-element.27), channel_id=1, source_target_pairs={{0,1},{1,2},{2,3},{3,4},{4,5},{5,6},{6,7},{7,8},{8,9},{9,10},{10,1... | collective-permute-start | bytes 4816904 | tf_op jit(solution)/shard_map/ppermute | solution.py:30
  10.3 3.9 %collective-permute-start.1 = (bf16[784,1024]{1,0:T(8,128)(2,1)S(1)}, bf16[784,1024]{1,0:T(8,128)(2,1)S(1)}, u32[]{:S(2)}, u32[]{:S(2)}) collective-permute-start(bf16[784,1024]{1,0:T(8,128)(2,1)S(1)} %get-tuple-element.28), channel_id=1, source_target_pairs={{1,0},{2,1},{3,2},{4,3},{5,4},{6,5},{7,6},{8,7},{9,8},{10,9},{11,1... | collective-permute-start | bytes 4816904 | tf_op jit(solution)/shard_map/ppermute | solution.py:30
  14.2 0.0 copy-done.1
  14.2 0.0 copy-start.4
  14.2 1.2 %shard_map.56 = (bf16[256,1024]{1,0:T(8,128)(2,1)S(1)}, bf16[256,1024]{1,0:T(8,128)(2,1)S(1)}, s32[2]{0:T(128)S(1)}) custom-call(s32[2]{0:T(128)S(1)} %get-tuple-element.25.flags, bf16[3,1024,1024]{2,1,0:T(8,128)(2,1)S(1)} %copy-done.1), custom_call_target="tpu_custom_call" | custom-call | bytes 2097152 | tf_op jit(solution)/shard_map/pallas_call | solution.py:157
  15.5 3.9 %collective-permute-start.2 = (bf16[256,1024]{1,0:T(8,128)(2,1)S(1)}, bf16[256,1024]{1,0:T(8,128)(2,1)S(1)}, u32[]{:S(2)}, u32[]{:S(2)}) collective-permute-start(bf16[256,1024]{1,0:T(8,128)(2,1)S(1)} %get-tuple-element.32), channel_id=1, source_target_pairs={{1,0},{2,1},{3,2},{4,3},{5,4},{6,5},{7,6},{8,7},{9,8},{10,9},{11,1... | collective-permute-start | bytes 1572872 | tf_op jit(solution)/shard_map/ppermute | solution.py:30
  19.4 1.9 %collective-permute-start.3 = (bf16[256,1024]{1,0:T(8,128)(2,1)S(1)}, bf16[256,1024]{1,0:T(8,128)(2,1)S(1)}, u32[]{:S(2)}, u32[]{:S(2)}) collective-permute-start(bf16[256,1024]{1,0:T(8,128)(2,1)S(1)} %get-tuple-element.35), channel_id=1, source_target_pairs={{0,1},{1,2},{2,3},{3,4},{4,5},{5,6},{6,7},{7,8},{8,9},{9,10},{10,1... | collective-permute-start | bytes 1572872 | tf_op jit(solution)/shard_map/ppermute | solution.py:30
  21.3 0.0 copy-done.4
  21.3 11.8 %shard_map.57 = (bf16[3,1024,1024]{2,1,0:T(8,128)(2,1)S(1)}, f32[3,1024]{1,0:T(4,128)S(1)}) custom-call(s32[1,2,6]{2,1,0:T(2,128)S(1)} %bitcast.3, s32[1]{0:T(128)S(6)} %copy.6.count, s32[2]{0:T(128)S(1)} %get-tuple-element.26.flags, bf16[3,1024,1024]{2,1,0:T(8,128)(2,1)S(1)} %copy-done.1, s32[3,1024]{1,0:T(4,128)S(1)} %get-tuple-element.24.keys), custom_call_target="tpu_custom_call" | custom-call | flops 12884901888 | bytes 12582912 | tf_op jit(solution)/shard_map/pallas_call | solution.py:210
  33.2 20.4 %collective-permute-done.raw_before = bf16[784,1024]{1,0:T(8,128)(2,1)S(1)} collective-permute-done((bf16[784,1024]{1,0:T(8,128)(2,1)S(1)}, bf16[784,1024]{1,0:T(8,128)(2,1)S(1)}, u32[]{:S(2)}, u32[]{:S(2)}) %collective-permute-start) | collective-permute-done | bytes 1605664 | tf_op jit(solution)/shard_map/ppermute | solution.py:30
  53.5 1.2 %collective-permute-done.1.raw_after = bf16[784,1024]{1,0:T(8,128)(2,1)S(1)} collective-permute-done((bf16[784,1024]{1,0:T(8,128)(2,1)S(1)}, bf16[784,1024]{1,0:T(8,128)(2,1)S(1)}, u32[]{:S(2)}, u32[]{:S(2)}) %collective-permute-start.1) | collective-permute-done | bytes 1605664 | tf_op jit(solution)/shard_map/ppermute | solution.py:30
  54.7 6.7 %shard_map.58 = (f32[1,768]{1,0:T(1,128)S(1)}, f32[1,768]{1,0:T(1,128)S(1)}, f32[3,1024]{1,0:T(4,128)S(1)}, s32[1,1024]{1,0:T(1,128)S(1)}, s32[1,1024]{1,0:T(1,128)S(1)}, /*index=5*/s32[2]{0:T(128)S(1)}) custom-call(s32[2]{0:T(128)S(1)} %get-tuple-element.26.flags, bf16[784,1024]{1,0:T(8,128)(2,1)S(1)} %collective-permute-done.raw_before, ...), custom_call_target="tpu_custom_call" | custom-call | flops 4831838208 | bytes 9437184 | tf_op jit(solution)/shard_map/pallas_call | solution.py:299
  61.4 0.0 collective-permute-done.3.raw
  61.5 0.7 shard_map.59
  62.1 10.6 %collective-permute-start.5 = (f32[1,1024]{1,0:T(1,128)S(1)}, f32[1,1024]{1,0:T(1,128)S(1)}, u32[]{:S(2)}, u32[]{:S(2)}) collective-permute-start(f32[1,1024]{1,0:T(1,128)S(1)} %get-tuple-element.42), channel_id=1, source_target_pairs={{1,0},{2,1},{3,2},{4,3},{5,4},{6,5},{7,6},{8,7},{9,8},{10,9},{11,1... | collective-permute-start | bytes 12296 | tf_op jit(solution)/shard_map/ppermute | solution.py:30
  72.8 0.0 collective-permute-done.2.raw
  72.8 2.7 %shard_map.60 = (f32[1,1024]{1,0:T(1,128)S(1)}, f32[3,1024]{1,0:T(4,128)S(1)}) custom-call(s32[2]{0:T(128)S(1)} %get-tuple-element.31.flags, bf16[256,1024]{1,0:T(8,128)(2,1)S(1)} %collective-permute-done.2.raw, s32[1,1024]{1,0:T(1,128)S(1)} %get-tuple-element.33.guest_keys, s32[3,1024]{1,0:T(4,128)S(1)} %get-tuple-element.24.keys, ...), custom_call_target="tpu_custom_call" | custom-call | flops 1073741824 | bytes 6815744 | tf_op jit(solution)/shard_map/pallas_call | solution.py:321
  75.5 1.9 %collective-permute-start.4 = (f32[1,1024]{1,0:T(1,128)S(1)}, f32[1,1024]{1,0:T(1,128)S(1)}, u32[]{:S(2)}, u32[]{:S(2)}) collective-permute-start(f32[1,1024]{1,0:T(1,128)S(1)} %get-tuple-element.41), channel_id=1, source_target_pairs={{0,1},{1,2},{2,3},{3,4},{4,5},{5,6},{6,7},{7,8},{8,9},{9,10},{10,1... | collective-permute-start | bytes 12296 | tf_op jit(solution)/shard_map/ppermute | solution.py:30
  77.5 0.1 pad.1.clone
  77.5 0.0 collective-permute-done.5
  77.5 4.1 %collective-permute-done.4 = f32[1,1024]{1,0:T(1,128)S(1)} collective-permute-done((f32[1,1024]{1,0:T(1,128)S(1)}, f32[1,1024]{1,0:T(1,128)S(1)}, u32[]{:S(2)}, u32[]{:S(2)}) %collective-permute-start.4) | collective-permute-done | bytes 4128 | tf_op jit(solution)/shard_map/ppermute | solution.py:30
  81.7 0.7 fusion
Async XLA Ops:
  0.7 2.8 %copy-start = (bf16[3,1024,1024]{2,1,0:T(8,128)(2,1)S(1)}, bf16[3,1024,1024]{2,1,0:T(8,128)(2,1)}, u32[]{:S(2)}) copy-start(bf16[3,1024,1024]{2,1,0:T(8,128)(2,1)} %raw.5) | copy-start | bytes 18874372
  3.4 0.7 copy-start.2
  4.2 0.7 copy-start.3
  4.8 0.7 copy-start.5
  5.5 8.7 %copy-start.1 = (bf16[3,1024,1024]{2,1,0:T(8,128)(2,1)S(1)}, bf16[3,1024,1024]{2,1,0:T(8,128)(2,1)}, u32[]{:S(2)}) copy-start(bf16[3,1024,1024]{2,1,0:T(8,128)(2,1)} %raw.5) | copy-start | bytes 18874372
  6.9 46.6 %collective-permute-start = (bf16[784,1024]{1,0:T(8,128)(2,1)S(1)}, bf16[784,1024]{1,0:T(8,128)(2,1)S(1)}, u32[]{:S(2)}, u32[]{:S(2)}) collective-permute-start(bf16[784,1024]{1,0:T(8,128)(2,1)S(1)} %get-tuple-element.27), channel_id=1, source_target_pairs={{0,1},{1,2},{2,3},{3,4},{4,5},{5,6},{6,7},{7,8},{8,9},{9,10},{10,1... | collective-permute-start | bytes 4816904 | tf_op jit(solution)/shard_map/ppermute | solution.py:30
  10.3 44.4 %collective-permute-start.1 = (bf16[784,1024]{1,0:T(8,128)(2,1)S(1)}, bf16[784,1024]{1,0:T(8,128)(2,1)S(1)}, u32[]{:S(2)}, u32[]{:S(2)}) collective-permute-start(bf16[784,1024]{1,0:T(8,128)(2,1)S(1)} %get-tuple-element.28), channel_id=1, source_target_pairs={{1,0},{2,1},{3,2},{4,3},{5,4},{6,5},{7,6},{8,7},{9,8},{10,9},{11,1... | collective-permute-start | bytes 4816904 | tf_op jit(solution)/shard_map/ppermute | solution.py:30
  14.2 7.1 %copy-start.4 = (s32[1,6,2]{1,2,0:T(2,128)S(1)}, s32[1,6,2]{1,2,0:T(2,128)}, u32[]{:S(2)}) copy-start(s32[1,6,2]{1,2,0:T(2,128)} %param.8) | copy-start | bytes 148
  15.5 57.3 %collective-permute-start.2 = (bf16[256,1024]{1,0:T(8,128)(2,1)S(1)}, bf16[256,1024]{1,0:T(8,128)(2,1)S(1)}, u32[]{:S(2)}, u32[]{:S(2)}) collective-permute-start(bf16[256,1024]{1,0:T(8,128)(2,1)S(1)} %get-tuple-element.32), channel_id=1, source_target_pairs={{1,0},{2,1},{3,2},{4,3},{5,4},{6,5},{7,6},{8,7},{9,8},{10,9},{11,1... | collective-permute-start | bytes 1572872 | tf_op jit(solution)/shard_map/ppermute | solution.py:30
  19.4 42.1 %collective-permute-start.3 = (bf16[256,1024]{1,0:T(8,128)(2,1)S(1)}, bf16[256,1024]{1,0:T(8,128)(2,1)S(1)}, u32[]{:S(2)}, u32[]{:S(2)}) collective-permute-start(bf16[256,1024]{1,0:T(8,128)(2,1)S(1)} %get-tuple-element.35), channel_id=1, source_target_pairs={{0,1},{1,2},{2,3},{3,4},{4,5},{5,6},{6,7},{7,8},{8,9},{9,10},{10,1... | collective-permute-start | bytes 1572872 | tf_op jit(solution)/shard_map/ppermute | solution.py:30
  62.1 15.4 %collective-permute-start.5 = (f32[1,1024]{1,0:T(1,128)S(1)}, f32[1,1024]{1,0:T(1,128)S(1)}, u32[]{:S(2)}, u32[]{:S(2)}) collective-permute-start(f32[1,1024]{1,0:T(1,128)S(1)} %get-tuple-element.42), channel_id=1, source_target_pairs={{1,0},{2,1},{3,2},{4,3},{5,4},{6,5},{7,6},{8,7},{9,8},{10,9},{11,1... | collective-permute-start | bytes 12296 | tf_op jit(solution)/shard_map/ppermute | solution.py:30
  75.5 6.1 %collective-permute-start.4 = (f32[1,1024]{1,0:T(1,128)S(1)}, f32[1,1024]{1,0:T(1,128)S(1)}, u32[]{:S(2)}, u32[]{:S(2)}) collective-permute-start(f32[1,1024]{1,0:T(1,128)S(1)} %get-tuple-element.41), channel_id=1, source_target_pairs={{0,1},{1,2},{2,3},{3,4},{4,5},{5,6},{6,7},{7,8},{8,9},{9,10},{10,1... | collective-permute-start | bytes 12296 | tf_op jit(solution)/shard_map/ppermute | solution.py:30
